TPU v7x, 32 devices: a whole 2x2x4 slice. The times are simulated.
32 devices in a mesh: dp: 2 (over core), expert: 16 (over z, y, x).
Axes of the slice: x: 2, y: 2, z: 4, core: 2. Of those that a mesh axis runs over, the one named last changes fastest.
Arguments:
- tokens: bfloat16 [4096, 4096], P(('dp', 'expert')), parts along dimension 0, may hold values from -6 to 6
- w_gate_up: bfloat16 [16, 2, 4096, 768], P('expert'), may hold values from -0.09375 to 0.09375
- w_down: bfloat16 [16, 768, 4096], P('expert'), may hold values from -0.21875 to 0.21875
- routes: int32 [4096, 8], P(('dp', 'expert')), parts along dimension 0, may hold values from 0 to 15, as said below
- gate_scaled: int32 [4096, 8], P(('dp', 'expert')), parts along dimension 0, may hold values from 1 to 1023
Outputs:
- mixed: bfloat16 [4096, 4096], P(('dp', 'expert')), parts along dimension 0
There are 2 independent parts, one for each index of `dp`. A program takes and returns all parts, laid end to end along the dimension named above; an argument that names none is the same for every part. Nothing has to cross between parts.
Inputs may be any that keep to these rules, and one draw needn't show every extreme that they name: `routes`: every row names 8 different experts. In each aligned block of 128 rows (the rows of one device) one expert, the same in every block, is named by exactly 128 rows; no other expert is named by more than 80 rows of a block, and a second expert, the same in every block, by exactly 80 rows of every block.
All inputs are finite; a program needn't handle non-finite values.
Results may differ from a plain program's by a relative error of at most 0.0057.
Values may be sent and summed in bfloat16 or wider, within the bound.
A program may use at most 192 MiB of HBM per device.

v0:
```python
import jax
import jax.numpy as jnp
from jax import lax
from jax.sharding import PartitionSpec as P


def from_root(block, axis, owner):
    block = jnp.where(lax.axis_index(axis) == owner, block, jnp.zeros_like(block))
    return lax.psum(block, axis)


def expert_rows(picked, gate_up, down_proj):
    gate_val = jnp.dot(picked, gate_up[0], preferred_element_type=jnp.float32)
    up_val = jnp.dot(picked, gate_up[1], preferred_element_type=jnp.float32)
    hidden = (jax.nn.silu(gate_val) * up_val).astype(jnp.bfloat16)
    return jnp.dot(hidden, down_proj, preferred_element_type=jnp.float32).astype(jnp.bfloat16)


def body(tokens, w_gate_up, w_down, routes, gate_scaled):
    experts = lax.axis_size("expert")
    tok_rows, model_width = tokens.shape
    top_count = routes.shape[1]
    cold_cap = 5 * tok_rows * top_count // (4 * experts)
    flat_routes = routes.reshape(-1)
    onehot = (flat_routes[:, None] == jnp.arange(experts, dtype=jnp.int32)[None, :]).astype(
        jnp.int32
    )
    before = jnp.cumsum(onehot, axis=0) - onehot
    ranked = jnp.sum(before * onehot, axis=1)
    gate_up = w_gate_up[0]
    down_proj = w_down[0]
    scaled = gate_scaled.astype(jnp.float32)
    weight = scaled / jnp.sum(scaled, axis=1, keepdims=True)
    counts = jnp.sum(onehot, axis=0)
    busiest = jnp.argmax(counts)
    hot_gate_up = from_root(gate_up, "expert", busiest)
    hot_down = from_root(down_proj, "expert", busiest)
    is_hot = flat_routes == busiest
    buffer_rows = experts * cold_cap
    slot_of = jnp.where(is_hot, buffer_rows, flat_routes * cold_cap + ranked)
    token_of = jnp.arange(flat_routes.shape[0], dtype=jnp.int32) // top_count
    source_rows = jnp.zeros((buffer_rows,), jnp.int32).at[slot_of].set(token_of, mode="drop")
    outgoing = jnp.take(tokens, source_rows, axis=0).reshape(experts, cold_cap, model_width)
    incoming = lax.all_to_all(outgoing, "expert", split_axis=0, concat_axis=0, tiled=True)
    slot_count = incoming.shape[1]
    expert_out = expert_rows(incoming.reshape(-1, model_width), gate_up, down_proj)
    expert_out = expert_out.reshape(experts, slot_count, model_width)
    returned_rows = lax.all_to_all(expert_out, "expert", split_axis=0, concat_axis=0, tiled=True)
    returned_rows = returned_rows.reshape(buffer_rows, model_width)
    gathered = jnp.take(returned_rows, jnp.minimum(slot_of, buffer_rows - 1), axis=0)
    gathered = gathered.reshape(tok_rows, top_count, model_width)
    local_out = expert_rows(tokens, hot_gate_up, hot_down)
    gathered = jnp.where(is_hot.reshape(tok_rows, top_count, 1), local_out[:, None, :], gathered)
    mixed = jnp.zeros((tok_rows, model_width), jnp.float32)
    for column in range(top_count):
        mixed = mixed + weight[:, column : column + 1] * gathered[:, column].astype(jnp.float32)
    return mixed.astype(jnp.bfloat16)


def solution(mesh):
    return jax.shard_map(
        body,
        mesh=mesh,
        in_specs=(
            P(("dp", "expert"), None),
            P("expert", None, None, None),
            P("expert", None, None),
            P(("dp", "expert"), None),
            P(("dp", "expert"), None),
        ),
        out_specs=P(("dp", "expert"), None),
        check_vma=False,
    )
```

profile of v0, /device:TPU:0, one launch (start us, length us, event | category | flops | bytes accessed | tf_op | source)
XLA Modules:
  0.0 1018.6 jit_solution(7963662137631653602)
XLA Ops:
  6.5 0.9 copy.18
  7.6 0.7 broadcast_multiply_fusion
  8.3 4.5 reduce-window.6
  13.2 0.1 fusion.35
  13.5 0.7 iota_reduce_fusion
  14.2 1.4 compare_and_fusion.1
  16.1 4.3 scatter_custom_fusion
  20.5 8.4 gather_fusion
  28.9 10.0 broadcast_select_fusion
  38.9 8.4 all-to-all-start
  47.3 0.2 all-reduce.3.cloned.1.call-start
  48.2 5.8 bitcast_select_fusion
  54.0 10.5 %select_bitcast_fusion = bf16[2,4096,768]{2,1,0:T(8,128)(2,1)} fusion(bf16[1,2,4096,768]{3,2,1,0:T(8,128)(2,1)} %param.6, pred[]{:T(512)S(6)} %eq.62), kind=kLoop, calls=%fused_computation.4 | loop fusion | flops 6291456 | bytes 25165824 | tf_op jit(solution)/shard_map/jit(_where)/select_n | solution.py:8
  64.5 291.4 %all-to-all-done = bf16[16,80,4096]{2,1,0:T(8,128)(2,1)} async-done(((bf16[16,80,4096]{2,1,0:T(8,128)(2,1)}), bf16[16,80,4096]{2,1,0:T(8,128)(2,1)}, u32[]{:S(2)}, u32[]{:S(2)}) %all-to-all-start) | async-done | bytes 10485792 | tf_op jit(solution)/shard_map/all_to_all | solution.py:44
  355.9 12.6 %fusion.5 = f32[1280,768]{1,0:T(8,128)S(1)} fusion(bf16[1280,4096]{1,0:T(8,128)(2,1)} %bitcast.12, bf16[1,2,4096,768]{3,2,1,0:T(8,128)(2,1)} %param.6), kind=kOutput, calls=%fused_computation.14 | convolution fusion | flops 8053063680 | bytes 20709376 | tf_op jit(solution)/shard_map/dot_general | solution.py:13
  368.6 13.3 %fusion.13 = bf16[1280,768]{1,0:T(8,128)(2,1)S(1)} fusion(bf16[1280,4096]{1,0:T(8,128)(2,1)} %bitcast.12, bf16[1,2,4096,768]{3,2,1,0:T(8,128)(2,1)} %param.6, f32[1280,768]{1,0:T(8,128)S(1)} %fusion.5), kind=kOutput, calls=%fused_computation.22 | convolution fusion | flops 8058961920 | bytes 22675456 | tf_op jit(solution)/shard_map/dot_general | solution.py:14
  381.9 10.5 %convolution_convert_fusion = bf16[1280,4096]{1,0:T(8,128)(2,1)} fusion(bf16[1280,768]{1,0:T(8,128)(2,1)S(1)} %fusion.13, bf16[1,768,4096]{2,1,0:T(8,128)(2,1)S(1)} %bitcast.126), kind=kOutput, calls=%fused_computation.3 | convolution fusion | flops 8058306560 | bytes 18743296 | tf_op jit(solution)/shard_map/dot_general | solution.py:16
  392.5 78.1 %all-to-all-start.1 = ((bf16[16,80,4096]{2,1,0:T(8,128)(2,1)}), bf16[16,80,4096]{2,1,0:T(8,128)(2,1)}, u32[]{:S(2)}, u32[]{:S(2)}) async-start(bf16[16,80,4096]{2,1,0:T(8,128)(2,1)} %bitcast.124), calls=%async_computation.1 | async-start | bytes 20971520 | tf_op jit(solution)/shard_map/all_to_all | solution.py:48
  470.7 488.0 %all-reduce.3.cloned.1.call-done = (bf16[768,4096]{1,0:T(8,128)(2,1)}, bf16[2,4096,768]{2,1,0:T(8,128)(2,1)}) async-done(((bf16[768,4096]{1,0:T(8,128)(2,1)}, bf16[2,4096,768]{2,1,0:T(8,128)(2,1)}), (bf16[768,4096]{1,0:T(8,128)(2,1)}, bf16[2,4096,768]{2,1,0:T(8,128)(2,1)})) %all-reduce.3.cloned.1.call-update) | async-done | bytes 18874384 | tf_op jit(solution)/shard_map/psum | solution.py:9
  958.6 4.6 fusion.24
  963.2 8.9 convolution_convert_fusion.1
  972.1 20.4 %gather_fusion.1 = bf16[1024,4096]{1,0:T(8,128)(2,1)} fusion(bf16[1280,4096]{1,0:T(8,128)(2,1)} %bitcast.16, s32[1024]{0:T(1024)S(1)} %broadcast_clamp_fusion), kind=kCustom, calls=%fused_computation.1 | custom fusion | bytes 16781312 | tf_op jit(solution)/shard_map/jit(_take)/gather | solution.py:50
  992.5 16.1 %fusion = bf16[128,8,4096]{2,0,1:T(8,128)(2,1)S(1)} fusion(bf16[128,8,4096]{2,1,0:T(8,128)(2,1)} %bitcast.123, pred[128,8]{0,1:T(8,128)(4,1)S(1)} %get-tuple-element.11, pred[128,8]{0,1:T(8,128)(4,1)S(1)} %get-tuple-element.12, bf16[128,4096]{1,0:T(8,128)(2,1)S(1)} %convolution_convert_fusion.1), kind=kLoop, calls=%fused_computation.7 | loop fusion | flops 8388608 | bytes 17827840 | tf_op jit(solution)/shard_map/jit(_where)/select_n | solution.py:53
  1008.6 3.1 fusion.17
  (36 shorter events, 1.4 us)
Async XLA Ops:
  6.5 14.0 %copy-start = (bf16[128,4096]{1,0:T(8,128)(2,1)S(1)}, bf16[128,4096]{1,0:T(8,128)(2,1)}, u32[]{:S(2)}) copy-start(bf16[128,4096]{1,0:T(8,128)(2,1)} %param.5) | copy-start | bytes 3145732
  38.9 317.0 %all-to-all-start = ((bf16[16,80,4096]{2,1,0:T(8,128)(2,1)}), bf16[16,80,4096]{2,1,0:T(8,128)(2,1)}, u32[]{:S(2)}, u32[]{:S(2)}) async-start(bf16[16,80,4096]{2,1,0:T(8,128)(2,1)} %broadcast_select_fusion), calls=%async_computation | async-start | bytes 20971520 | tf_op jit(solution)/shard_map/all_to_all | solution.py:44
  47.3 911.3 %all-reduce.3.cloned.1.call-start = ((), (), s32[]{:S(2)}) async-start(), calls=%async_computation.2 | async-start | bytes 37748736 | tf_op jit(solution)/shard_map/psum | solution.py:9
  355.9 26.0 %slice-start = ((s8[6291456]{0:T(1024)(128)(4,1)}), s8[4194304]{0:T(1024)(128)(4,1)S(1)}, s32[]{:S(2)}) async-start(s8[6291456]{0:T(1024)(128)(4,1)} %bitcast.125), calls=%async_computation.3 | async-start | bytes 8388608
  368.6 13.3 %slice-start.1 = ((s8[6291456]{0:T(1024)(128)(4,1)}), s8[2097152]{0:T(1024)(128)(4,1)S(1)}, s32[]{:S(2)}) async-start(s8[6291456]{0:T(1024)(128)(4,1)} %bitcast.125), calls=%async_computation.4 | async-start | bytes 4194304
  392.5 78.1 %copy-start.1 = (s32[128,8]{0,1:T(8,128)S(1)}, s32[128,8]{0,1:T(8,128)}, u32[]{:S(2)}) copy-start(s32[128,8]{0,1:T(8,128)} %param.9) | copy-start | bytes 12292
  392.5 579.7 %all-to-all-start.1 = ((bf16[16,80,4096]{2,1,0:T(8,128)(2,1)}), bf16[16,80,4096]{2,1,0:T(8,128)(2,1)}, u32[]{:S(2)}, u32[]{:S(2)}) async-start(bf16[16,80,4096]{2,1,0:T(8,128)(2,1)} %bitcast.124), calls=%async_computation.1 | async-start | bytes 20971520 | tf_op jit(solution)/shard_map/all_to_all | solution.py:48
Sparse Core Ops, SparseCore 0:
  64.6 893.9 all-reduce.2
where the time goes:
time: 1020 us
  waiting for transfers between devices  779 us (76%)
  starting transfers between devices  86.7 us (8%)
  other arithmetic  53.2 us (5%)
  matrix products  50 us (5%)
  local copies, waits for them, and re-layouts  35.1 us (3%)
  between operations  14.3 us (1%)
    psum x1, waiting for transfers between devices, from_root(): return lax.psum(block, axis)  488 us
    all_to_all x1, waiting for transfers between devices, body(): lax.all_to_all(outgoing, 'expert', split_axis=0, concat_axis=0, tiled=True)  291 us
    all_to_all x1, starting transfers between devices, body(): lax.all_to_all(expert_out, 'expert', split_axis=0, concat_axis=0, tiled=T...  78.1 us
  transfers between devices with their start and end apart: 3, of which 2 were waited for; matrix products, arithmetic and copies ran while one was open for 7% of the time, Pallas kernels for 0%

commit v1 on v0

v1 whole, which is shorter than its diff:
```python
import jax
import jax.numpy as jnp
from jax import lax
from jax.sharding import PartitionSpec as P

CHUNKS = 2


def expert_rows(picked, gate_up, down_proj):
    gate_val = jnp.dot(picked, gate_up[0], preferred_element_type=jnp.float32)
    up_val = jnp.dot(picked, gate_up[1], preferred_element_type=jnp.float32)
    hidden = (jax.nn.silu(gate_val) * up_val).astype(jnp.bfloat16)
    return jnp.dot(hidden, down_proj, preferred_element_type=jnp.float32).astype(jnp.bfloat16)


def body(tokens, w_gate_up, w_down, routes, gate_scaled):
    experts = lax.axis_size("expert")
    tok_rows, model_width = tokens.shape
    gate_up = w_gate_up[0]
    down_proj = w_down[0]
    scaled = gate_scaled.astype(jnp.float32)
    weight = scaled / jnp.sum(scaled, axis=1, keepdims=True)
    names = jnp.arange(experts, dtype=jnp.int32)[:, None, None]
    share = jnp.sum(jnp.where(routes[None] == names, weight[None], 0.0), axis=2)
    share = lax.all_to_all(share, "expert", split_axis=0, concat_axis=0, tiled=True)
    rows = tok_rows // CHUNKS
    mixed = []
    for chunk in range(CHUNKS):
        part = slice(chunk * rows, (chunk + 1) * rows)
        gathered = lax.all_gather(tokens[part], "expert", axis=0, tiled=True)
        expert_out = expert_rows(gathered, gate_up, down_proj)
        scale = share[:, part].reshape(-1, 1)
        weighted = (scale * expert_out.astype(jnp.float32)).astype(jnp.bfloat16)
        mixed.append(lax.psum_scatter(weighted, "expert", scatter_dimension=0, tiled=True))
    return jnp.concatenate(mixed, axis=0)


def solution(mesh):
    return jax.shard_map(
        body,
        mesh=mesh,
        in_specs=(
            P(("dp", "expert"), None),
            P("expert", None, None, None),
            P("expert", None, None),
            P(("dp", "expert"), None),
            P(("dp", "expert"), None),
        ),
        out_specs=P(("dp", "expert"), None),
        check_vma=False,
    )
```

time: 1020 us -> 611 us (0.60)
  waiting for transfers between devices: 779 us -> 508 us
  starting transfers between devices: 86.7 us -> 0.3 us
  other arithmetic: 53.2 us -> 4.37 us
  local copies, waits for them, and re-layouts: 35.1 us -> 2.48 us
  blocking collectives: 0 us -> 15.4 us
  matrix products: 50 us -> 65 us
    psum x1 -> x0, waiting for transfers between devices: 488 us -> none  [from_root(): return lax.psum(block, axis)]
    reduce_scatter x0 -> x2, waiting for transfers between devices: none -> 328 us  [body(): lax.psum_scatter(weighted, 'expert', scatter_dimension=0, tiled=True)]
    all_to_all x2 -> x0, waiting for transfers between devices: 291 us -> none  [the longest x1 291 us: body(): lax.all_to_all(outgoing, 'expert', split_axis=0, concat_axis=0, tiled=True)]
    all_gather x0 -> x2, waiting for transfers between devices: none -> 179 us  [body(): gathered = lax.all_gather(tokens[part], 'expert', axis=0, tiled=True)]
    all_to_all x2 -> x0, starting transfers between devices: 86.5 us -> none  [the longest x1 78.1 us: body(): lax.all_to_all(expert_out, 'expert', split_axis=0, concat_axis=0, tiled=T...]
    select_n x7 -> x0, other arithmetic: 42.4 us -> none  [the longest x2 16.3 us: from_root(): jnp.where(lax.axis_index(axis) == owner, block, jnp.zeros_like(block))]
    gather x2 -> x0, local copies, waits for them, and re-layouts: 28.8 us -> none  [the longest x1 20.4 us: body(): jnp.take(returned_rows, jnp.minimum(slot_of, buffer_rows - 1), axis=0)]
    all_to_all x0 -> x1, blocking collectives: none -> 15.4 us  [body(): lax.all_to_all(share, 'expert', split_axis=0, concat_axis=0, tiled=True)]
  transfers between devices with their start and end apart: 3 -> 4, of which waited for: 2 -> 4; matrix products, arithmetic and copies ran while one was open for 7% -> 11% of each run, Pallas kernels for 0% -> 0%
where the time goes in v1:
time: 611 us; the launch traced here: 609 us
  waiting for transfers between devices  508 us (83%)
  matrix products  65 us (11%)
  blocking collectives  15.4 us (3%)
  between operations  13.2 us (2%)
    reduce_scatter x2, waiting for transfers between devices, body(): lax.psum_scatter(weighted, 'expert', scatter_dimension=0, tiled=True)  328 us
    all_gather x2, waiting for transfers between devices, body(): gathered = lax.all_gather(tokens[part], 'expert', axis=0, tiled=True)  179 us
    dot_general x2, matrix products, expert_rows(): jnp.dot(hidden, down_proj, preferred_element_type=jnp.float32)  23.4 us
    dot_general x2, matrix products, expert_rows(): up_val = jnp.dot(picked, gate_up[1], preferred_element_type=jnp.float32)  22.1 us
    dot_general x2, matrix products, expert_rows(): gate_val = jnp.dot(picked, gate_up[0], preferred_element_type=jnp.float32)  19.6 us
    all_to_all x1, blocking collectives, body(): lax.all_to_all(share, 'expert', split_axis=0, concat_axis=0, tiled=True)  15.4 us
  transfers between devices with their start and end apart: 4, of which 4 were waited for; matrix products, arithmetic and copies ran while one was open for 11% of the time, Pallas kernels for 0%

profile of v1, /device:TPU:0, one launch (start us, length us, event | category | flops | bytes accessed | tf_op | source)
XLA Modules:
  0.0 609.1 jit_solution(12020782251007288541)
XLA Ops:
  6.5 2.3 fusion.18
  8.8 0.0 all-gather.5.cloned.1.call-start
  8.9 0.7 all-gather.5.cloned.1.call-update
  9.6 0.0 reduce-scatter.3.cloned.1.call-start
  9.6 0.7 convert_reduce_fusion
  10.3 0.7 convert_divide_fusion
  11.0 0.7 select_reduce_fusion
  11.7 15.4 %all_to_all.12 = f32[16,1,128]{2,1,0:T(1,128)S(1)} all-to-all(f32[16,1,128]{2,1,0:T(1,128)S(1)} %bitcast.30), channel_id=1, replica_groups=mesh['dp'=2,'expert'=16] {'expert'}, dimensions={0} | all-to-all | bytes 16384 | tf_op jit(solution)/shard_map/all_to_all | solution.py:25
  27.1 0.1 fusion.19
  27.2 0.1 mul.33
  27.3 98.4 %all-gather.3.cloned.1.call-done = bf16[1024,4096]{1,0:T(8,128)(2,1)} async-done(((bf16[64,4096]{1,0:T(8,128)(2,1)}), bf16[1024,4096]{1,0:T(8,128)(2,1)}) %all-gather.3.cloned.1.call-update) | async-done | bytes 8388624 | tf_op jit(solution)/shard_map/all_gather | solution.py:30
  125.7 11.0 %fusion.4 = f32[1024,768]{1,0:T(8,128)S(1)} fusion(bf16[1024,4096]{1,0:T(8,128)(2,1)} %all-gather.3.cloned.1.call-done, bf16[1,2,4096,768]{3,2,1,0:T(8,128)(2,1)} %param.6), kind=kOutput, calls=%fused_computation.6 | convolution fusion | flops 6442450944 | bytes 17825792 | tf_op jit(solution)/shard_map/dot_general | solution.py:11
  136.7 9.8 %multiply_convert_fusion.3 = bf16[1024,768]{1,0:T(8,128)(2,1)S(1)} fusion(f32[1024,768]{1,0:T(8,128)S(1)} %fusion.4, bf16[1024,4096]{1,0:T(8,128)(2,1)S(1)} %copy-done.1, bf16[1,2,4096,768]{3,2,1,0:T(8,128)(2,1)} %param.6), kind=kOutput, calls=%fused_computation.17 | convolution fusion | flops 6447169536 | bytes 19398656 | tf_op jit(solution)/shard_map/dot_general | solution.py:10
  146.5 11.7 %multiply_convert_fusion.1 = bf16[1024,4096]{1,0:T(8,128)(2,1)} fusion(f32[1024]{0:T(1024)S(1)} %mul.33, bf16[1024,768]{1,0:T(8,128)(2,1)S(1)} %multiply_convert_fusion.3, bf16[1,768,4096]{2,1,0:T(8,128)(2,1)} %param.7), kind=kOutput, calls=%fused_computation.1 | convolution fusion | flops 6459228160 | bytes 16257024 | tf_op jit(solution)/shard_map/dot_general | solution.py:13
  158.3 0.0 reduce-scatter.3.cloned.1.call-update
  158.3 0.2 reduce-scatter.5.cloned.1.call-start
  158.5 0.1 mul.38
  158.6 81.0 %all-gather.5.cloned.1.call-done = bf16[1024,4096]{1,0:T(8,128)(2,1)} async-done(((bf16[64,4096]{1,0:T(8,128)(2,1)}), bf16[1024,4096]{1,0:T(8,128)(2,1)}) %all-gather.5.cloned.1.call-update) | async-done | bytes 8388624 | tf_op jit(solution)/shard_map/all_gather | solution.py:30
  239.5 11.0 %fusion.2 = f32[1024,768]{1,0:T(8,128)S(1)} fusion(bf16[1024,4096]{1,0:T(8,128)(2,1)} %all-gather.5.cloned.1.call-done, bf16[1,2,4096,768]{3,2,1,0:T(8,128)(2,1)} %param.6), kind=kOutput, calls=%fused_computation.4 | convolution fusion | flops 6442450944 | bytes 17825792 | tf_op jit(solution)/shard_map/dot_general | solution.py:11
  250.6 9.8 %multiply_convert_fusion.2 = bf16[1024,768]{1,0:T(8,128)(2,1)S(1)} fusion(f32[1024,768]{1,0:T(8,128)S(1)} %fusion.2, bf16[1024,4096]{1,0:T(8,128)(2,1)S(1)} %copy-done, bf16[1,2,4096,768]{3,2,1,0:T(8,128)(2,1)} %param.6), kind=kOutput, calls=%fused_computation.16 | convolution fusion | flops 6447169536 | bytes 19398656 | tf_op jit(solution)/shard_map/dot_general | solution.py:10
  260.4 11.7 %multiply_convert_fusion = bf16[1024,4096]{1,0:T(8,128)(2,1)} fusion(f32[1024]{0:T(1024)S(1)} %mul.38, bf16[1024,768]{1,0:T(8,128)(2,1)S(1)} %multiply_convert_fusion.2, bf16[1,768,4096]{2,1,0:T(8,128)(2,1)} %param.7), kind=kOutput, calls=%fused_computation | convolution fusion | flops 6459228160 | bytes 16257024 | tf_op jit(solution)/shard_map/dot_general | solution.py:13
  272.1 145.8 %reduce-scatter.3.cloned.1.call-done = bf16[64,4096]{1,0:T(8,128)(2,1)} async-done(((bf16[1024,4096]{1,0:T(8,128)(2,1)}), bf16[64,4096]{1,0:T(8,128)(2,1)}) %reduce-scatter.3.cloned.1.call-update) | async-done | bytes 524304 | tf_op jit(solution)/shard_map/reduce_scatter | solution.py:34
  417.9 182.4 %reduce-scatter.5.cloned.1.call-done = bf16[64,4096]{1,0:T(8,128)(2,1)} async-done(((bf16[1024,4096]{1,0:T(8,128)(2,1)}), bf16[64,4096]{1,0:T(8,128)(2,1)}) %reduce-scatter.5.cloned.1.call-update) | async-done | bytes 524304 | tf_op jit(solution)/shard_map/reduce_scatter | solution.py:34
  600.3 2.3 pad_maximum_fusion
  (7 shorter events, 0.0 us)
Async XLA Ops:
  6.5 119.2 %all-gather.3.cloned.1.call-start = ((), (), s32[]{:S(2)}) async-start(), calls=%async_computation.3 | async-start | bytes 8912896 | tf_op jit(solution)/shard_map/all_gather | solution.py:30
  8.8 230.7 %all-gather.5.cloned.1.call-start = ((), (), s32[]{:S(2)}) async-start(), calls=%async_computation.5 | async-start | bytes 8912896 | tf_op jit(solution)/shard_map/all_gather | solution.py:30
  9.6 408.3 %reduce-scatter.3.cloned.1.call-start = ((), (), s32[]{:S(2)}) async-start(), calls=%async_computation.4 | async-start | bytes 8912896 | tf_op jit(solution)/shard_map/reduce_scatter | solution.py:34
  125.7 11.0 %copy-start.1 = (bf16[1024,4096]{1,0:T(8,128)(2,1)S(1)}, bf16[1024,4096]{1,0:T(8,128)(2,1)}, u32[]{:S(2)}) copy-start(bf16[1024,4096]{1,0:T(8,128)(2,1)} %all-gather.3.cloned.1.call-done) | copy-start | bytes 25165828
  158.3 442.0 %reduce-scatter.5.cloned.1.call-start = ((), (), s32[]{:S(2)}) async-start(), calls=%async_computation.6 | async-start | bytes 8912896 | tf_op jit(solution)/shard_map/reduce_scatter | solution.py:34
  239.5 11.1 %copy-start = (bf16[1024,4096]{1,0:T(8,128)(2,1)S(1)}, bf16[1024,4096]{1,0:T(8,128)(2,1)}, u32[]{:S(2)}) copy-start(bf16[1024,4096]{1,0:T(8,128)(2,1)} %all-gather.5.cloned.1.call-done) | copy-start | bytes 25165828
Sparse Core Ops, SparseCore 0:
  10.1 115.5 all-gather.2
  128.5 111.0 all-gather.4
  241.8 176.0 reduce-scatter.2
  420.1 180.2 reduce-scatter.4

commit v2 on v1

--- a/solution.py
+++ b/solution.py
@@ -6,11 +6,28 @@
 CHUNKS = 2
 
 
-def expert_rows(picked, gate_up, down_proj):
+def hidden_rows(picked, gate_up):
     gate_val = jnp.dot(picked, gate_up[0], preferred_element_type=jnp.float32)
     up_val = jnp.dot(picked, gate_up[1], preferred_element_type=jnp.float32)
-    hidden = (jax.nn.silu(gate_val) * up_val).astype(jnp.bfloat16)
-    return jnp.dot(hidden, down_proj, preferred_element_type=jnp.float32).astype(jnp.bfloat16)
+    return (jax.nn.silu(gate_val) * up_val).astype(jnp.bfloat16)
+
+
+def halving_sum(blocks, order):
+    experts = blocks.shape[0]
+    bits = experts.bit_length() - 1
+    me = lax.axis_index("expert")
+    data = blocks.reshape((2,) * bits + blocks.shape[1:])
+    left = list(range(bits - 1, -1, -1))
+    for bit in order:
+        axis = left.index(bit)
+        left.remove(bit)
+        mine = (me >> bit) & 1
+        keep = lax.dynamic_index_in_dim(data, mine, axis, keepdims=False)
+        send = lax.dynamic_index_in_dim(data, 1 - mine, axis, keepdims=False)
+        swap = [(device, device ^ (1 << bit)) for device in range(experts)]
+        came = lax.ppermute(send, "expert", swap)
+        data = (keep.astype(jnp.float32) + came.astype(jnp.float32)).astype(blocks.dtype)
+    return data
 
 
 def body(tokens, w_gate_up, w_down, routes, gate_scaled):
@@ -24,14 +41,28 @@
     share = jnp.sum(jnp.where(routes[None] == names, weight[None], 0.0), axis=2)
     share = lax.all_to_all(share, "expert", split_axis=0, concat_axis=0, tiled=True)
     rows = tok_rows // CHUNKS
+    bits = experts.bit_length() - 1
+    far = list(range(bits - 1, 1, -1))
+    eighth = model_width // 8
+    groups = (
+        (0, 3 * eighth, [0, 1] + far),
+        (3 * eighth, 6 * eighth, [1, 0] + far),
+        (6 * eighth, model_width, [2, 0, 1] + far[:-1]),
+    )
     mixed = []
     for chunk in range(CHUNKS):
         part = slice(chunk * rows, (chunk + 1) * rows)
         gathered = lax.all_gather(tokens[part], "expert", axis=0, tiled=True)
-        expert_out = expert_rows(gathered, gate_up, down_proj)
+        hidden = hidden_rows(gathered, gate_up)
         scale = share[:, part].reshape(-1, 1)
-        weighted = (scale * expert_out.astype(jnp.float32)).astype(jnp.bfloat16)
-        mixed.append(lax.psum_scatter(weighted, "expert", scatter_dimension=0, tiled=True))
+        columns = []
+        for start, stop, order in groups:
+            expert_out = jnp.dot(
+                hidden, down_proj[:, start:stop], preferred_element_type=jnp.float32
+            ).astype(jnp.bfloat16)
+            weighted = (scale * expert_out.astype(jnp.float32)).astype(jnp.bfloat16)
+            columns.append(halving_sum(weighted.reshape(experts, rows, stop - start), order))
+        mixed.append(jnp.concatenate(columns, axis=1))
     return jnp.concatenate(mixed, axis=0)
 
 

time: 611 us -> 508 us (0.83); the launches traced: 609 us -> 499 us
  waiting for transfers between devices: 508 us -> 353 us
  starting transfers between devices: 0.3 us -> 53.8 us
  blocking collectives: 15.4 us -> 0 us
    reduce_scatter x2 -> x0, waiting for transfers between devices: 328 us -> none  [body(): lax.psum_scatter(weighted, 'expert', scatter_dimension=0, tiled=True)]
    ppermute x0 -> x24, waiting for transfers between devices: none -> 162 us  [halving_sum(): came = lax.ppermute(send, 'expert', swap)]
    ppermute x0 -> x24, starting transfers between devices: none -> 45.5 us  [halving_sum(): came = lax.ppermute(send, 'expert', swap)]
    all_to_all x1 -> x0, blocking collectives: 15.4 us -> none  [body(): lax.all_to_all(share, 'expert', split_axis=0, concat_axis=0, tiled=True)]
    all_to_all x0 -> x1, starting transfers between devices: none -> 8.31 us  [body(): lax.all_to_all(share, 'expert', split_axis=0, concat_axis=0, tiled=True)]
    all_to_all x0 -> x1, waiting for transfers between devices: none -> 7.27 us  [body(): lax.all_to_all(share, 'expert', split_axis=0, concat_axis=0, tiled=True)]
    dot_general x6 -> x10, matrix products: 65 us -> 65.3 us  [the longest x6 23.5 us: body(): jnp.dot(hidden, down_proj[:, start:stop], preferred_element_type=jnp.floa...]
  transfers between devices with their start and end apart: 4 -> 27, of which waited for: 4 -> 16; matrix products, arithmetic and copies ran while one was open for 11% -> 9% of each run, Pallas kernels for 0% -> 0%
where the time goes in v2:
time: 508 us; the launch traced here: 499 us
  waiting for transfers between devices  353 us (69%)
  matrix products  65.3 us (13%)
  starting transfers between devices  53.8 us (11%)
  between operations  14 us (3%)
  local copies, waits for them, and re-layouts  6.99 us (1%)
  other arithmetic  6.23 us (1%)
    all_gather x2, waiting for transfers between devices, body(): gathered = lax.all_gather(tokens[part], 'expert', axis=0, tiled=True)  183 us
    ppermute x24, waiting for transfers between devices, halving_sum(): came = lax.ppermute(send, 'expert', swap)  162 us
    ppermute x24, starting transfers between devices, halving_sum(): came = lax.ppermute(send, 'expert', swap)  45.5 us
    dot_general x6, matrix products, body(): jnp.dot(hidden, down_proj[:, start:stop], preferred_element_type=jnp.floa...  23.5 us
    dot_general x2, matrix products, hidden_rows(): up_val = jnp.dot(picked, gate_up[1], preferred_element_type=jnp.float32)  22.1 us
    dot_general x2, matrix products, hidden_rows(): gate_val = jnp.dot(picked, gate_up[0], preferred_element_type=jnp.float32)  19.7 us
  transfers between devices with their start and end apart: 27, of which 16 were waited for; matrix products, arithmetic and copies ran while one was open for 9% of the time, Pallas kernels for 0%

profile of v2, /device:TPU:0, one launch (start us, length us, event | category | flops | bytes accessed | tf_op | source)
XLA Modules:
  0.0 499.1 jit_solution(16308442185408672930)
XLA Ops:
  10.3 8.3 %all-to-all-start = ((f32[16,1,128]{2,1,0:T(1,128)}), f32[16,1,128]{2,1,0:T(1,128)S(1)}, u32[]{:S(2)}, u32[]{:S(2)}) async-start(f32[16,1,128]{2,1,0:T(1,128)} %bitcast.1), calls=%async_computation | async-start | bytes 16384 | tf_op jit(solution)/shard_map/all_to_all | solution.py:42
  18.6 7.3 %all-to-all-done = f32[16,1,128]{2,1,0:T(1,128)S(1)} async-done(((f32[16,1,128]{2,1,0:T(1,128)}), f32[16,1,128]{2,1,0:T(1,128)S(1)}, u32[]{:S(2)}, u32[]{:S(2)}) %all-to-all-start) | async-done | bytes 8224 | tf_op jit(solution)/shard_map/all_to_all | solution.py:42
  26.1 99.6 %all-gather.5.cloned.1.call-done = bf16[1024,4096]{1,0:T(8,128)(2,1)} async-done(((bf16[64,4096]{1,0:T(8,128)(2,1)}), bf16[1024,4096]{1,0:T(8,128)(2,1)}) %all-gather.5.cloned.1.call-update) | async-done | bytes 8388624 | tf_op jit(solution)/shard_map/all_gather | solution.py:55
  125.7 11.0 %fusion = f32[1024,768]{1,0:T(8,128)S(1)} fusion(bf16[1024,4096]{1,0:T(8,128)(2,1)} %all-gather.5.cloned.1.call-done, bf16[1,2,4096,768]{3,2,1,0:T(8,128)(2,1)} %param.6), kind=kOutput, calls=%fused_computation | convolution fusion | flops 6442450944 | bytes 17825792 | tf_op jit(solution)/shard_map/dot_general | solution.py:11
  136.8 9.8 %multiply_convert_fusion.6 = bf16[1024,768]{1,0:T(8,128)(2,1)S(1)} fusion(f32[1024,768]{1,0:T(8,128)S(1)} %fusion, bf16[1024,4096]{1,0:T(8,128)(2,1)S(1)} %copy-done.3, bf16[1,2,4096,768]{3,2,1,0:T(8,128)(2,1)} %param.6), kind=kOutput, calls=%fused_computation.30 | convolution fusion | flops 6447169536 | bytes 19398656 | tf_op jit(solution)/shard_map/dot_general | solution.py:10
  146.6 5.1 %multiply_convert_fusion.4 = bf16[1024,1024]{1,0:T(8,128)(2,1)} fusion(f32[1024]{0:T(1024)S(1)} %mul.69, bf16[1024,768]{1,0:T(8,128)(2,1)S(1)} %multiply_convert_fusion.6, bf16[768,4096]{1,0:T(8,128)(2,1)} %bitcast.185), kind=kOutput, calls=%fused_computation.16 | convolution fusion | flops 1614807040 | bytes 5246976 | tf_op jit(solution)/shard_map/dot_general | solution.py:60
  151.7 4.5 multiply_convert_fusion
  156.2 83.4 %all-gather.3.cloned.1.call-done = bf16[1024,4096]{1,0:T(8,128)(2,1)} async-done(((bf16[64,4096]{1,0:T(8,128)(2,1)}), bf16[1024,4096]{1,0:T(8,128)(2,1)}) %all-gather.3.cloned.1.call-update) | async-done | bytes 8388624 | tf_op jit(solution)/shard_map/all_gather | solution.py:55
  239.6 11.0 %fusion.2 = f32[1024,768]{1,0:T(8,128)S(1)} fusion(bf16[1024,4096]{1,0:T(8,128)(2,1)} %all-gather.3.cloned.1.call-done, bf16[1,2,4096,768]{3,2,1,0:T(8,128)(2,1)} %param.6), kind=kOutput, calls=%fused_computation.2 | convolution fusion | flops 6442450944 | bytes 17825792 | tf_op jit(solution)/shard_map/dot_general | solution.py:11
  250.6 9.9 %multiply_convert_fusion.7 = bf16[1024,768]{1,0:T(8,128)(2,1)S(1)} fusion(f32[1024,768]{1,0:T(8,128)S(1)} %fusion.2, bf16[1024,4096]{1,0:T(8,128)(2,1)S(1)} %copy-done.4, bf16[1,2,4096,768]{3,2,1,0:T(8,128)(2,1)} %param.6), kind=kOutput, calls=%fused_computation.31 | convolution fusion | flops 6447169536 | bytes 19398656 | tf_op jit(solution)/shard_map/dot_general | solution.py:10
  260.6 3.8 multiply_convert_fusion.5
  274.1 4.5 multiply_convert_fusion.3
  280.9 13.4 %collective-permute-done.20 = bf16[2,2,2,64,1024]{4,3,0,1,2:T(8,128)(2,1)S(1)} collective-permute-done((bf16[2,2,2,64,1024]{4,3,0,1,2:T(8,128)(2,1)S(1)}, bf16[2,2,2,64,1024]{4,3,0,1,2:T(8,128)(2,1)S(1)}, u32[]{:S(2)}, u32[]{:S(2)}) %collective-permute-start.20) | collective-permute-done | bytes 1048608 | tf_op jit(solution)/shard_map/ppermute | solution.py:28
  299.4 15.3 %collective-permute-done.8 = bf16[2,2,2,64,1024]{4,3,0,1,2:T(8,128)(2,1)S(1)} collective-permute-done((bf16[2,2,2,64,1024]{4,3,0,1,2:T(8,128)(2,1)}, bf16[2,2,2,64,1024]{4,3,0,1,2:T(8,128)(2,1)S(1)}, u32[]{:S(2)}, u32[]{:S(2)}) %collective-permute-start.8) | collective-permute-done | bytes 1048608 | tf_op jit(solution)/shard_map/ppermute | solution.py:28
  319.7 23.7 %collective-permute-done.12 = bf16[2,2,2,64,1536]{4,3,1,0,2:T(8,128)(2,1)S(1)} collective-permute-done((bf16[2,2,2,64,1536]{4,3,1,0,2:T(8,128)(2,1)S(1)}, bf16[2,2,2,64,1536]{4,3,1,0,2:T(8,128)(2,1)S(1)}, u32[]{:S(2)}, u32[]{:S(2)}) %collective-permute-start.12) | collective-permute-done | bytes 1572896 | tf_op jit(solution)/shard_map/ppermute | solution.py:28
  345.2 43.2 %collective-permute-done.9 = bf16[2,2,64,1024]{3,2,0,1:T(8,128)(2,1)S(1)} collective-permute-done((bf16[2,2,64,1024]{3,2,0,1:T(8,128)(2,1)S(1)}, bf16[2,2,64,1024]{3,2,0,1:T(8,128)(2,1)S(1)}, u32[]{:S(2)}, u32[]{:S(2)}) %collective-permute-start.9) | collective-permute-done | bytes 524320 | tf_op jit(solution)/shard_map/ppermute | solution.py:28
  393.9 18.3 %collective-permute-done.10 = bf16[2,64,1024]{2,1,0:T(8,128)(2,1)S(1)} collective-permute-done((bf16[2,64,1024]{2,1,0:T(8,128)(2,1)S(1)}, bf16[2,64,1024]{2,1,0:T(8,128)(2,1)S(1)}, u32[]{:S(2)}, u32[]{:S(2)}) %collective-permute-start.10) | collective-permute-done | bytes 262176 | tf_op jit(solution)/shard_map/ppermute | solution.py:28
  415.3 5.7 %collective-permute-done.23 = bf16[64,1024]{1,0:T(8,128)(2,1)S(1)} collective-permute-done((bf16[64,1024]{1,0:T(8,128)(2,1)S(1)}, bf16[64,1024]{1,0:T(8,128)(2,1)S(1)}, u32[]{:S(2)}, u32[]{:S(2)}) %collective-permute-start.23) | collective-permute-done | bytes 131104 | tf_op jit(solution)/shard_map/ppermute | solution.py:28
  422.7 5.7 %collective-permute-done.11 = bf16[64,1024]{1,0:T(8,128)(2,1)S(1)} collective-permute-done((bf16[64,1024]{1,0:T(8,128)(2,1)S(1)}, bf16[64,1024]{1,0:T(8,128)(2,1)S(1)}, u32[]{:S(2)}, u32[]{:S(2)}) %collective-permute-start.11) | collective-permute-done | bytes 131104 | tf_op jit(solution)/shard_map/ppermute | solution.py:28
  435.6 20.1 %collective-permute-done.18 = bf16[2,64,1536]{2,1,0:T(8,128)(2,1)S(1)} collective-permute-done((bf16[2,64,1536]{2,1,0:T(8,128)(2,1)S(1)}, bf16[2,64,1536]{2,1,0:T(8,128)(2,1)S(1)}, u32[]{:S(2)}, u32[]{:S(2)}) %collective-permute-start.18) | collective-permute-done | bytes 393248 | tf_op jit(solution)/shard_map/ppermute | solution.py:28
  455.8 10.4 %collective-permute-start.19 = (bf16[64,1536]{1,0:T(8,128)(2,1)S(1)}, bf16[64,1536]{1,0:T(8,128)(2,1)S(1)}, u32[]{:S(2)}, u32[]{:S(2)}) collective-permute-start(bf16[64,1536]{1,0:T(8,128)(2,1)S(1)} %dynamic-slice_bitcast_fusion.12), channel_id=1, source_target_pairs={{0,4},{1,5},{2,6},{3,7},{4,0},{5,1},{6,2},{7,3},{8,12},{9,13},{10,... | collective-permute-start | bytes 589832 | tf_op jit(solution)/shard_map/ppermute | solution.py:28
  466.7 8.0 %collective-permute-start.15 = (bf16[64,1536]{1,0:T(8,128)(2,1)S(1)}, bf16[64,1536]{1,0:T(8,128)(2,1)S(1)}, u32[]{:S(2)}, u32[]{:S(2)}) collective-permute-start(bf16[64,1536]{1,0:T(8,128)(2,1)S(1)} %dynamic-slice_bitcast_fusion.13), channel_id=1, source_target_pairs={{0,4},{1,5},{2,6},{3,7},{4,0},{5,1},{6,2},{7,3},{8,12},{9,13},{10,... | collective-permute-start | bytes 589832 | tf_op jit(solution)/shard_map/ppermute | solution.py:28
  474.6 6.4 %collective-permute-done.6 = bf16[2,64,1536]{2,1,0:T(8,128)(2,1)S(1)} collective-permute-done((bf16[2,64,1536]{2,1,0:T(8,128)(2,1)S(1)}, bf16[2,64,1536]{2,1,0:T(8,128)(2,1)S(1)}, u32[]{:S(2)}, u32[]{:S(2)}) %collective-permute-start.6) | collective-permute-done | bytes 393248 | tf_op jit(solution)/shard_map/ppermute | solution.py:28
  481.3 4.0 collective-permute-done.2
  (124 shorter events, 52.6 us)
Async XLA Ops:
  6.5 119.2 %all-gather.5.cloned.1.call-start = ((), (), s32[]{:S(2)}) async-start(), calls=%async_computation.2 | async-start | bytes 8912896 | tf_op jit(solution)/shard_map/all_gather | solution.py:55
  8.8 230.7 %all-gather.3.cloned.1.call-start = ((), (), s32[]{:S(2)}) async-start(), calls=%async_computation.1 | async-start | bytes 8912896 | tf_op jit(solution)/shard_map/all_gather | solution.py:55
  10.3 15.6 %all-to-all-start = ((f32[16,1,128]{2,1,0:T(1,128)}), f32[16,1,128]{2,1,0:T(1,128)S(1)}, u32[]{:S(2)}, u32[]{:S(2)}) async-start(f32[16,1,128]{2,1,0:T(1,128)} %bitcast.1), calls=%async_computation | async-start | bytes 16384 | tf_op jit(solution)/shard_map/all_to_all | solution.py:42
  268.1 26.2 %collective-permute-start.20 = (bf16[2,2,2,64,1024]{4,3,0,1,2:T(8,128)(2,1)S(1)}, bf16[2,2,2,64,1024]{4,3,0,1,2:T(8,128)(2,1)S(1)}, u32[]{:S(2)}, u32[]{:S(2)}) collective-permute-start(bf16[2,2,2,64,1024]{4,3,0,1,2:T(8,128)(2,1)S(1)} %bitcast.183), channel_id=1, source_target_pairs={{0,4},{1,5},{2,6},{3,7},{4,0},{5,1},{6,2},{7,3},{8,12},{9,13},{10,... | collective-permute-start | bytes 3145736 | tf_op jit(solution)/shard_map/ppermute | solution.py:28
  272.6 42.2 %collective-permute-start.8 = (bf16[2,2,2,64,1024]{4,3,0,1,2:T(8,128)(2,1)}, bf16[2,2,2,64,1024]{4,3,0,1,2:T(8,128)(2,1)S(1)}, u32[]{:S(2)}, u32[]{:S(2)}) collective-permute-start(bf16[2,2,2,64,1024]{4,3,0,1,2:T(8,128)(2,1)} %bitcast.172), channel_id=1, source_target_pairs={{0,4},{1,5},{2,6},{3,7},{4,0},{5,1},{6,2},{7,3},{8,12},{9,13},{10,... | collective-permute-start | bytes 3145736 | tf_op jit(solution)/shard_map/ppermute | solution.py:28
  279.4 38.2 %collective-permute-start.16 = (bf16[2,2,2,64,1536]{4,3,1,0,2:T(8,128)(2,1)S(1)}, bf16[2,2,2,64,1536]{4,3,1,0,2:T(8,128)(2,1)S(1)}, u32[]{:S(2)}, u32[]{:S(2)}) collective-permute-start(bf16[2,2,2,64,1536]{4,3,1,0,2:T(8,128)(2,1)S(1)} %bitcast.181), channel_id=1, source_target_pairs={{0,2},{1,3},{2,0},{3,1},{4,6},{5,7},{6,4},{7,5},{8,10},{9,11},{10,... | collective-permute-start | bytes 4718600 | tf_op jit(solution)/shard_map/ppermute | solution.py:28
  294.8 21.8 %collective-permute-start.21 = (bf16[2,2,64,1024]{3,2,0,1:T(8,128)(2,1)S(1)}, bf16[2,2,64,1024]{3,2,0,1:T(8,128)(2,1)S(1)}, u32[]{:S(2)}, u32[]{:S(2)}) collective-permute-start(bf16[2,2,64,1024]{3,2,0,1:T(8,128)(2,1)S(1)} %dynamic-slice_bitcast_fusion.4), channel_id=1, source_target_pairs={{0,1},{1,0},{2,3},{3,2},{4,5},{5,4},{6,7},{7,6},{8,9},{9,8},{10,11... | collective-permute-start | bytes 1572872 | tf_op jit(solution)/shard_map/ppermute | solution.py:28
  296.9 46.5 %collective-permute-start.12 = (bf16[2,2,2,64,1536]{4,3,1,0,2:T(8,128)(2,1)S(1)}, bf16[2,2,2,64,1536]{4,3,1,0,2:T(8,128)(2,1)S(1)}, u32[]{:S(2)}, u32[]{:S(2)}) collective-permute-start(bf16[2,2,2,64,1536]{4,3,1,0,2:T(8,128)(2,1)S(1)} %bitcast.182), channel_id=1, source_target_pairs={{0,1},{1,0},{2,3},{3,2},{4,5},{5,4},{6,7},{7,6},{8,9},{9,8},{10,11... | collective-permute-start | bytes 4718600 | tf_op jit(solution)/shard_map/ppermute | solution.py:28
  297.8 92.3 %collective-permute-start.4 = (bf16[2,2,2,64,1536]{4,3,1,0,2:T(8,128)(2,1)S(1)}, bf16[2,2,2,64,1536]{4,3,1,0,2:T(8,128)(2,1)S(1)}, u32[]{:S(2)}, u32[]{:S(2)}) collective-permute-start(bf16[2,2,2,64,1536]{4,3,1,0,2:T(8,128)(2,1)S(1)} %bitcast.180), channel_id=1, source_target_pairs={{0,2},{1,3},{2,0},{3,1},{4,6},{5,7},{6,4},{7,5},{8,10},{9,11},{10,... | collective-permute-start | bytes 4718600 | tf_op jit(solution)/shard_map/ppermute | solution.py:28
  314.8 76.4 %collective-permute-start = (bf16[2,2,2,64,1536]{4,3,1,0,2:T(8,128)(2,1)S(1)}, bf16[2,2,2,64,1536]{4,3,1,0,2:T(8,128)(2,1)S(1)}, u32[]{:S(2)}, u32[]{:S(2)}) collective-permute-start(bf16[2,2,2,64,1536]{4,3,1,0,2:T(8,128)(2,1)S(1)} %bitcast.179), channel_id=1, source_target_pairs={{0,1},{1,0},{2,3},{3,2},{4,5},{5,4},{6,7},{7,6},{8,9},{9,8},{10,11... | collective-permute-start | bytes 4718600 | tf_op jit(solution)/shard_map/ppermute | solution.py:28
  316.6 71.8 %collective-permute-start.9 = (bf16[2,2,64,1024]{3,2,0,1:T(8,128)(2,1)S(1)}, bf16[2,2,64,1024]{3,2,0,1:T(8,128)(2,1)S(1)}, u32[]{:S(2)}, u32[]{:S(2)}) collective-permute-start(bf16[2,2,64,1024]{3,2,0,1:T(8,128)(2,1)S(1)} %dynamic-slice_bitcast_fusion.5), channel_id=1, source_target_pairs={{0,1},{1,0},{2,3},{3,2},{4,5},{5,4},{6,7},{7,6},{8,9},{9,8},{10,11... | collective-permute-start | bytes 1572872 | tf_op jit(solution)/shard_map/ppermute | solution.py:28
  317.6 75.4 %collective-permute-start.22 = (bf16[2,64,1024]{2,1,0:T(8,128)(2,1)S(1)}, bf16[2,64,1024]{2,1,0:T(8,128)(2,1)S(1)}, u32[]{:S(2)}, u32[]{:S(2)}) collective-permute-start(bf16[2,64,1024]{2,1,0:T(8,128)(2,1)S(1)} %dynamic-slice_bitcast_fusion.10), channel_id=1, source_target_pairs={{0,2},{1,3},{2,0},{3,1},{4,6},{5,7},{6,4},{7,5},{8,10},{9,11},{10,... | collective-permute-start | bytes 786440 | tf_op jit(solution)/shard_map/ppermute | solution.py:28
  343.4 85.0 %collective-permute-start.17 = (bf16[2,2,64,1536]{3,2,1,0:T(8,128)(2,1)S(1)}, bf16[2,2,64,1536]{3,2,1,0:T(8,128)(2,1)S(1)}, u32[]{:S(2)}, u32[]{:S(2)}) collective-permute-start(bf16[2,2,64,1536]{3,2,1,0:T(8,128)(2,1)S(1)} %dynamic-slice_bitcast_fusion), channel_id=1, source_target_pairs={{0,1},{1,0},{2,3},{3,2},{4,5},{5,4},{6,7},{7,6},{8,9},{9,8},{10,11... | collective-permute-start | bytes 2359304 | tf_op jit(solution)/shard_map/ppermute | solution.py:28
  388.3 42.0 %collective-permute-start.13 = (bf16[2,2,64,1536]{3,2,1,0:T(8,128)(2,1)S(1)}, bf16[2,2,64,1536]{3,2,1,0:T(8,128)(2,1)S(1)}, u32[]{:S(2)}, u32[]{:S(2)}) collective-permute-start(bf16[2,2,64,1536]{3,2,1,0:T(8,128)(2,1)S(1)} %dynamic-slice_bitcast_fusion.1), channel_id=1, source_target_pairs={{0,2},{1,3},{2,0},{3,1},{4,6},{5,7},{6,4},{7,5},{8,10},{9,11},{10,... | collective-permute-start | bytes 2359304 | tf_op jit(solution)/shard_map/ppermute | solution.py:28
  390.1 22.2 %collective-permute-start.10 = (bf16[2,64,1024]{2,1,0:T(8,128)(2,1)S(1)}, bf16[2,64,1024]{2,1,0:T(8,128)(2,1)S(1)}, u32[]{:S(2)}, u32[]{:S(2)}) collective-permute-start(bf16[2,64,1024]{2,1,0:T(8,128)(2,1)S(1)} %dynamic-slice_bitcast_fusion.11), channel_id=1, source_target_pairs={{0,2},{1,3},{2,0},{3,1},{4,6},{5,7},{6,4},{7,5},{8,10},{9,11},{10,... | collective-permute-start | bytes 786440 | tf_op jit(solution)/shard_map/ppermute | solution.py:28
  391.2 40.8 %collective-permute-start.5 = (bf16[2,2,64,1536]{3,2,1,0:T(8,128)(2,1)S(1)}, bf16[2,2,64,1536]{3,2,1,0:T(8,128)(2,1)S(1)}, u32[]{:S(2)}, u32[]{:S(2)}) collective-permute-start(bf16[2,2,64,1536]{3,2,1,0:T(8,128)(2,1)S(1)} %dynamic-slice_bitcast_fusion.2), channel_id=1, source_target_pairs={{0,1},{1,0},{2,3},{3,2},{4,5},{5,4},{6,7},{7,6},{8,9},{9,8},{10,11... | collective-permute-start | bytes 2359304 | tf_op jit(solution)/shard_map/ppermute | solution.py:28
  393.0 40.9 %collective-permute-start.1 = (bf16[2,2,64,1536]{3,2,1,0:T(8,128)(2,1)S(1)}, bf16[2,2,64,1536]{3,2,1,0:T(8,128)(2,1)S(1)}, u32[]{:S(2)}, u32[]{:S(2)}) collective-permute-start(bf16[2,2,64,1536]{3,2,1,0:T(8,128)(2,1)S(1)} %dynamic-slice_bitcast_fusion.3), channel_id=1, source_target_pairs={{0,2},{1,3},{2,0},{3,1},{4,6},{5,7},{6,4},{7,5},{8,10},{9,11},{10,... | collective-permute-start | bytes 2359304 | tf_op jit(solution)/shard_map/ppermute | solution.py:28
  412.2 8.8 %collective-permute-start.23 = (bf16[64,1024]{1,0:T(8,128)(2,1)S(1)}, bf16[64,1024]{1,0:T(8,128)(2,1)S(1)}, u32[]{:S(2)}, u32[]{:S(2)}) collective-permute-start(bf16[64,1024]{1,0:T(8,128)(2,1)S(1)} %dynamic-slice_bitcast_fusion.16), channel_id=1, source_target_pairs={{0,8},{1,9},{2,10},{3,11},{4,12},{5,13},{6,14},{7,15},{8,0},{9,1},... | collective-permute-start | bytes 393224 | tf_op jit(solution)/shard_map/ppermute | solution.py:28
  428.7 27.0 %collective-permute-start.18 = (bf16[2,64,1536]{2,1,0:T(8,128)(2,1)S(1)}, bf16[2,64,1536]{2,1,0:T(8,128)(2,1)S(1)}, u32[]{:S(2)}, u32[]{:S(2)}) collective-permute-start(bf16[2,64,1536]{2,1,0:T(8,128)(2,1)S(1)} %dynamic-slice_bitcast_fusion.6), channel_id=1, source_target_pairs={{0,8},{1,9},{2,10},{3,11},{4,12},{5,13},{6,14},{7,15},{8,0},{9,1},... | collective-permute-start | bytes 1179656 | tf_op jit(solution)/shard_map/ppermute | solution.py:28
  430.6 35.9 %collective-permute-start.14 = (bf16[2,64,1536]{2,1,0:T(8,128)(2,1)S(1)}, bf16[2,64,1536]{2,1,0:T(8,128)(2,1)S(1)}, u32[]{:S(2)}, u32[]{:S(2)}) collective-permute-start(bf16[2,64,1536]{2,1,0:T(8,128)(2,1)S(1)} %dynamic-slice_bitcast_fusion.7), channel_id=1, source_target_pairs={{0,8},{1,9},{2,10},{3,11},{4,12},{5,13},{6,14},{7,15},{8,0},{9,1},... | collective-permute-start | bytes 1179656 | tf_op jit(solution)/shard_map/ppermute | solution.py:28
  432.3 48.8 %collective-permute-start.6 = (bf16[2,64,1536]{2,1,0:T(8,128)(2,1)S(1)}, bf16[2,64,1536]{2,1,0:T(8,128)(2,1)S(1)}, u32[]{:S(2)}, u32[]{:S(2)}) collective-permute-start(bf16[2,64,1536]{2,1,0:T(8,128)(2,1)S(1)} %dynamic-slice_bitcast_fusion.8), channel_id=1, source_target_pairs={{0,8},{1,9},{2,10},{3,11},{4,12},{5,13},{6,14},{7,15},{8,0},{9,1},... | collective-permute-start | bytes 1179656 | tf_op jit(solution)/shard_map/ppermute | solution.py:28
  434.2 51.1 %collective-permute-start.2 = (bf16[2,64,1536]{2,1,0:T(8,128)(2,1)S(1)}, bf16[2,64,1536]{2,1,0:T(8,128)(2,1)S(1)}, u32[]{:S(2)}, u32[]{:S(2)}) collective-permute-start(bf16[2,64,1536]{2,1,0:T(8,128)(2,1)S(1)} %dynamic-slice_bitcast_fusion.9), channel_id=1, source_target_pairs={{0,8},{1,9},{2,10},{3,11},{4,12},{5,13},{6,14},{7,15},{8,0},{9,1},... | collective-permute-start | bytes 1179656 | tf_op jit(solution)/shard_map/ppermute | solution.py:28
  455.8 29.7 %collective-permute-start.19 = (bf16[64,1536]{1,0:T(8,128)(2,1)S(1)}, bf16[64,1536]{1,0:T(8,128)(2,1)S(1)}, u32[]{:S(2)}, u32[]{:S(2)}) collective-permute-start(bf16[64,1536]{1,0:T(8,128)(2,1)S(1)} %dynamic-slice_bitcast_fusion.12), channel_id=1, source_target_pairs={{0,4},{1,5},{2,6},{3,7},{4,0},{5,1},{6,2},{7,3},{8,12},{9,13},{10,... | collective-permute-start | bytes 589832 | tf_op jit(solution)/shard_map/ppermute | solution.py:28
  466.7 18.9 %collective-permute-start.15 = (bf16[64,1536]{1,0:T(8,128)(2,1)S(1)}, bf16[64,1536]{1,0:T(8,128)(2,1)S(1)}, u32[]{:S(2)}, u32[]{:S(2)}) collective-permute-start(bf16[64,1536]{1,0:T(8,128)(2,1)S(1)} %dynamic-slice_bitcast_fusion.13), channel_id=1, source_target_pairs={{0,4},{1,5},{2,6},{3,7},{4,0},{5,1},{6,2},{7,3},{8,12},{9,13},{10,... | collective-permute-start | bytes 589832 | tf_op jit(solution)/shard_map/ppermute | solution.py:28
  (14 other events, 106.5 us)
Sparse Core Ops, SparseCore 0:
  10.1 115.5 all-gather.4
  128.5 111.0 all-gather.2

commit v3 on v2

--- a/solution.py
+++ b/solution.py
@@ -30,6 +30,21 @@
     return data
 
 
+def doubling_gather(rows, order):
+    experts = lax.axis_size("expert")
+    me = lax.axis_index("expert")
+    data = rows
+    held = []
+    for bit in reversed(order):
+        swap = [(device, device ^ (1 << bit)) for device in range(experts)]
+        came = lax.ppermute(data, "expert", swap)
+        first = ((me >> bit) & 1) == 0
+        held = sorted(held + [bit], reverse=True)
+        pair = [jnp.where(first, data, came), jnp.where(first, came, data)]
+        data = jnp.stack(pair, axis=held.index(bit))
+    return data.reshape(experts * rows.shape[0], rows.shape[1])
+
+
 def body(tokens, w_gate_up, w_down, routes, gate_scaled):
     experts = lax.axis_size("expert")
     tok_rows, model_width = tokens.shape
@@ -52,7 +67,9 @@
     mixed = []
     for chunk in range(CHUNKS):
         part = slice(chunk * rows, (chunk + 1) * rows)
-        gathered = lax.all_gather(tokens[part], "expert", axis=0, tiled=True)
+        gathered = jnp.concatenate(
+            [doubling_gather(tokens[part, start:stop], order) for start, stop, order in groups], axis=1
+        )
         hidden = hidden_rows(gathered, gate_up)
         scale = share[:, part].reshape(-1, 1)
         columns = []

time: 508 us -> 475 us (0.935)
  waiting for transfers between devices: 353 us -> 305 us
  between operations: 14 us -> 1.37 us
  other arithmetic: 6.23 us -> 17.7 us
  starting transfers between devices: 53.8 us -> 64.4 us
    all_gather x2 -> x0, waiting for transfers between devices: 183 us -> none  [body(): gathered = lax.all_gather(tokens[part], 'expert', axis=0, tiled=True)]
    ppermute x0 -> x24, waiting for transfers between devices: none -> 125 us  [doubling_gather(): came = lax.ppermute(data, 'expert', swap)]
    ppermute x0 -> x24, starting transfers between devices: none -> 29.1 us  [doubling_gather(): came = lax.ppermute(data, 'expert', swap)]
    ppermute x24, starting transfers between devices: 45.5 us -> 27 us  [halving_sum(): came = lax.ppermute(send, 'expert', swap)]
    ppermute x24, waiting for transfers between devices: 162 us -> 179 us  [halving_sum(): came = lax.ppermute(send, 'expert', swap)]
    another operation x0 -> x45, other arithmetic: none -> 9.25 us  [doubling_gather(): data = jnp.stack(pair, axis=held.index(bit))]
    all_to_all x1, waiting for transfers between devices: 7.27 us -> 0.95 us  [body(): lax.all_to_all(share, 'expert', split_axis=0, concat_axis=0, tiled=True)]
  transfers between devices with their start and end apart: 27 -> 49, of which waited for: 16 -> 32; matrix products, arithmetic and copies ran while one was open for 9% -> 12% of each run, Pallas kernels for 0% -> 0%
where the time goes in v3:
time: 475 us; the launch traced here: 465 us
  waiting for transfers between devices  305 us (64%)
  matrix products  66.4 us (14%)
  starting transfers between devices  64.4 us (14%)
  other arithmetic  17.7 us (4%)
  local copies, waits for them, and re-layouts  10.6 us (2%)
    ppermute x24, waiting for transfers between devices, halving_sum(): came = lax.ppermute(send, 'expert', swap)  179 us
    ppermute x24, waiting for transfers between devices, doubling_gather(): came = lax.ppermute(data, 'expert', swap)  125 us
    ppermute x24, starting transfers between devices, doubling_gather(): came = lax.ppermute(data, 'expert', swap)  29.1 us
    ppermute x24, starting transfers between devices, halving_sum(): came = lax.ppermute(send, 'expert', swap)  27 us
    dot_general x2, matrix products, hidden_rows(): up_val = jnp.dot(picked, gate_up[1], preferred_element_type=jnp.float32)  22.6 us
    dot_general x2, matrix products, hidden_rows(): gate_val = jnp.dot(picked, gate_up[0], preferred_element_type=jnp.float32)  22.3 us
    dot_general x6, matrix products, body(): jnp.dot(hidden, down_proj[:, start:stop], preferred_element_type=jnp.floa...  21.6 us
  transfers between devices with their start and end apart: 49, of which 32 were waited for; matrix products, arithmetic and copies ran while one was open for 12% of the time, Pallas kernels for 0%

profile of v3, /device:TPU:0, one launch (start us, length us, event | category | flops | bytes accessed | tf_op | source)
XLA Modules:
  0.0 465.5 jit_solution(15888452868657547461)
XLA Ops:
  2.8 8.3 %all-to-all-start = ((f32[16,1,128]{2,1,0:T(1,128)}), f32[16,1,128]{2,1,0:T(1,128)S(1)}, u32[]{:S(2)}, u32[]{:S(2)}) async-start(f32[16,1,128]{2,1,0:T(1,128)} %bitcast.1), calls=%async_computation | async-start | bytes 16384 | tf_op jit(solution)/shard_map/all_to_all | solution.py:57
  29.7 11.5 %collective-permute-done.32 = bf16[64,1024]{1,0:T(8,128)(2,1)S(1)} collective-permute-done((bf16[64,1024]{1,0:T(8,128)(2,1)S(1)}, bf16[64,1024]{1,0:T(8,128)(2,1)S(1)}, u32[]{:S(2)}, u32[]{:S(2)}) %collective-permute-start.32) | collective-permute-done | bytes 131104 | tf_op jit(solution)/shard_map/ppermute | solution.py:40
  56.9 29.6 %collective-permute-done.5 = bf16[2,64,1536]{2,1,0:T(8,128)(2,1)S(1)} collective-permute-done((bf16[2,64,1536]{2,1,0:T(8,128)(2,1)S(1)}, bf16[2,64,1536]{2,1,0:T(8,128)(2,1)S(1)}, u32[]{:S(2)}, u32[]{:S(2)}) %collective-permute-start.5) | collective-permute-done | bytes 393248 | tf_op jit(solution)/shard_map/ppermute | solution.py:40
  87.2 7.7 %collective-permute-done.25 = bf16[2,64,1536]{2,1,0:T(8,128)(2,1)S(1)} collective-permute-done((bf16[2,64,1536]{2,1,0:T(8,128)(2,1)S(1)}, bf16[2,64,1536]{2,1,0:T(8,128)(2,1)S(1)}, u32[]{:S(2)}, u32[]{:S(2)}) %collective-permute-start.25) | collective-permute-done | bytes 393248 | tf_op jit(solution)/shard_map/ppermute | solution.py:40
  96.4 6.8 %collective-permute-done.29 = bf16[2,64,1536]{2,1,0:T(8,128)(2,1)S(1)} collective-permute-done((bf16[2,64,1536]{2,1,0:T(8,128)(2,1)S(1)}, bf16[2,64,1536]{2,1,0:T(8,128)(2,1)S(1)}, u32[]{:S(2)}, u32[]{:S(2)}) %collective-permute-start.29) | collective-permute-done | bytes 393248 | tf_op jit(solution)/shard_map/ppermute | solution.py:40
  108.5 6.9 %collective-permute-done.6 = bf16[2,2,64,1536]{3,2,1,0:T(8,128)(2,1)S(1)} collective-permute-done((bf16[2,2,64,1536]{3,2,1,0:T(8,128)(2,1)S(1)}, bf16[2,2,64,1536]{3,2,1,0:T(8,128)(2,1)S(1)}, u32[]{:S(2)}, u32[]{:S(2)}) %collective-permute-start.6) | collective-permute-done | bytes 786464 | tf_op jit(solution)/shard_map/ppermute | solution.py:40
  117.1 5.8 %collective-permute-done.26 = bf16[2,2,64,1536]{3,2,1,0:T(8,128)(2,1)S(1)} collective-permute-done((bf16[2,2,64,1536]{3,2,1,0:T(8,128)(2,1)S(1)}, bf16[2,2,64,1536]{3,2,1,0:T(8,128)(2,1)S(1)}, u32[]{:S(2)}, u32[]{:S(2)}) %collective-permute-start.26) | collective-permute-done | bytes 786464 | tf_op jit(solution)/shard_map/ppermute | solution.py:40
  123.7 8.5 %collective-permute-done.30 = bf16[2,2,64,1536]{3,2,1,0:T(8,128)(2,1)S(1)} collective-permute-done((bf16[2,2,64,1536]{3,2,1,0:T(8,128)(2,1)S(1)}, bf16[2,2,64,1536]{3,2,1,0:T(8,128)(2,1)S(1)}, u32[]{:S(2)}, u32[]{:S(2)}) %collective-permute-start.30) | collective-permute-done | bytes 786464 | tf_op jit(solution)/shard_map/ppermute | solution.py:40
  134.9 18.0 %collective-permute-done.35 = bf16[2,2,2,64,1024]{4,3,2,1,0:T(8,128)(2,1)S(1)} collective-permute-done((bf16[2,2,2,64,1024]{4,3,2,1,0:T(8,128)(2,1)S(1)}, bf16[2,2,2,64,1024]{4,3,2,1,0:T(8,128)(2,1)S(1)}, u32[]{:S(2)}, u32[]{:S(2)}) %collective-permute-start.35) | collective-permute-done | bytes 1048608 | tf_op jit(solution)/shard_map/ppermute | solution.py:40
  154.8 11.1 %collective-permute-done.3 = bf16[2,2,2,64,1536]{4,3,2,1,0:T(8,128)(2,1)S(1)} collective-permute-done((bf16[2,2,2,64,1536]{4,3,2,1,0:T(8,128)(2,1)S(1)}, bf16[2,2,2,64,1536]{4,3,2,1,0:T(8,128)(2,1)S(1)}, u32[]{:S(2)}, u32[]{:S(2)}) %collective-permute-start.3) | collective-permute-done | bytes 1572896 | tf_op jit(solution)/shard_map/ppermute | solution.py:40
  167.1 11.2 %fusion.6 = f32[1024,768]{1,0:T(8,128)} fusion(bf16[1,2,4096,768]{3,2,1,0:T(8,128)(2,1)} %param.6, bf16[1024,1024]{1,0:T(8,128)(2,1)S(1)} %bitcast.309, bf16[1024,1536]{1,0:T(8,128)(2,1)S(1)} %bitcast.297, bf16[1024,1536]{1,0:T(8,128)(2,1)S(1)} %bitcast.295), kind=kOutput, calls=%fused_computation.8 | convolution fusion | flops 6467616768 | bytes 17825792 | tf_op jit(solution)/shard_map/dot_general | solution.py:10
  178.3 11.9 %multiply_convert_fusion.7 = bf16[1024,768]{1,0:T(8,128)(2,1)} fusion(f32[1024,768]{1,0:T(8,128)} %fusion.6, bf16[1,2,4096,768]{3,2,1,0:T(8,128)(2,1)} %param.6, bf16[1024,1024]{1,0:T(8,128)(2,1)S(1)} %bitcast.310, bf16[1024,1536]{1,0:T(8,128)(2,1)S(1)} %bitcast.298, bf16[1024,1536]{1,0:T(8,128)(2,1)S(1)} %bitcast.296), kind=kOutput, calls=%fused_computation.37 | convolution fusion | flops 6472335360 | bytes 19398656 | tf_op jit(solution)/shard_map/dot_general | solution.py:11
  190.2 8.3 %collective-permute-done.27 = bf16[2,2,2,64,1536]{4,3,2,1,0:T(8,128)(2,1)} collective-permute-done((bf16[2,2,2,64,1536]{4,3,2,1,0:T(8,128)(2,1)S(1)}, bf16[2,2,2,64,1536]{4,3,2,1,0:T(8,128)(2,1)}, u32[]{:S(2)}, u32[]{:S(2)}) %collective-permute-start.27) | collective-permute-done | bytes 1572896 | tf_op jit(solution)/shard_map/ppermute | solution.py:40
  215.3 11.1 %fusion.4 = f32[1024,768]{1,0:T(8,128)} fusion(bf16[1,2,4096,768]{3,2,1,0:T(8,128)(2,1)} %param.6, bf16[1024,1024]{1,0:T(8,128)(2,1)S(1)} %bitcast.308, bf16[1024,1536]{1,0:T(8,128)(2,1)S(1)} %bitcast.299, bf16[1024,1536]{1,0:T(8,128)(2,1)S(1)} %bitcast.293), kind=kOutput, calls=%fused_computation.6 | convolution fusion | flops 6467616768 | bytes 17825792 | tf_op jit(solution)/shard_map/dot_general | solution.py:10
  226.4 10.6 %multiply_convert_fusion.6 = bf16[1024,768]{1,0:T(8,128)(2,1)S(1)} fusion(f32[1024,768]{1,0:T(8,128)} %fusion.4, bf16[1,2,4096,768]{3,2,1,0:T(8,128)(2,1)} %param.6, bf16[1024,1024]{1,0:T(8,128)(2,1)} %bitcast.307, bf16[1024,1536]{1,0:T(8,128)(2,1)S(1)} %bitcast.300, bf16[1024,1536]{1,0:T(8,128)(2,1)S(1)} %bitcast.294), kind=kOutput, calls=%fused_computation.36 | convolution fusion | flops 6472335360 | bytes 19398656 | tf_op jit(solution)/shard_map/dot_general | solution.py:11
  256.9 18.0 %collective-permute-done.20 = bf16[2,2,2,64,1024]{4,3,0,1,2:T(8,128)(2,1)S(1)} collective-permute-done((bf16[2,2,2,64,1024]{4,3,0,1,2:T(8,128)(2,1)S(1)}, bf16[2,2,2,64,1024]{4,3,0,1,2:T(8,128)(2,1)S(1)}, u32[]{:S(2)}, u32[]{:S(2)}) %collective-permute-start.20) | collective-permute-done | bytes 1048608 | tf_op jit(solution)/shard_map/ppermute | solution.py:28
  276.0 19.0 %collective-permute-done.44 = bf16[2,2,2,64,1024]{4,3,0,1,2:T(8,128)(2,1)S(1)} collective-permute-done((bf16[2,2,2,64,1024]{4,3,0,1,2:T(8,128)(2,1)S(1)}, bf16[2,2,2,64,1024]{4,3,0,1,2:T(8,128)(2,1)S(1)}, u32[]{:S(2)}, u32[]{:S(2)}) %collective-permute-start.44) | collective-permute-done | bytes 1048608 | tf_op jit(solution)/shard_map/ppermute | solution.py:28
  296.5 31.0 %collective-permute-done.21 = bf16[2,2,64,1024]{3,2,0,1:T(8,128)(2,1)S(1)} collective-permute-done((bf16[2,2,64,1024]{3,2,0,1:T(8,128)(2,1)S(1)}, bf16[2,2,64,1024]{3,2,0,1:T(8,128)(2,1)S(1)}, u32[]{:S(2)}, u32[]{:S(2)}) %collective-permute-start.21) | collective-permute-done | bytes 524320 | tf_op jit(solution)/shard_map/ppermute | solution.py:28
  328.3 8.4 %collective-permute-done.45 = bf16[2,2,64,1024]{3,2,0,1:T(8,128)(2,1)S(1)} collective-permute-done((bf16[2,2,64,1024]{3,2,0,1:T(8,128)(2,1)S(1)}, bf16[2,2,64,1024]{3,2,0,1:T(8,128)(2,1)S(1)}, u32[]{:S(2)}, u32[]{:S(2)}) %collective-permute-start.45) | collective-permute-done | bytes 524320 | tf_op jit(solution)/shard_map/ppermute | solution.py:28
  342.7 22.1 %collective-permute-done.40 = bf16[2,2,2,64,1536]{4,3,1,0,2:T(8,128)(2,1)S(1)} collective-permute-done((bf16[2,2,2,64,1536]{4,3,1,0,2:T(8,128)(2,1)S(1)}, bf16[2,2,2,64,1536]{4,3,1,0,2:T(8,128)(2,1)S(1)}, u32[]{:S(2)}, u32[]{:S(2)}) %collective-permute-start.40) | collective-permute-done | bytes 1572896 | tf_op jit(solution)/shard_map/ppermute | solution.py:28
  376.1 14.0 %collective-permute-done.23 = bf16[64,1024]{1,0:T(8,128)(2,1)S(1)} collective-permute-done((bf16[64,1024]{1,0:T(8,128)(2,1)S(1)}, bf16[64,1024]{1,0:T(8,128)(2,1)S(1)}, u32[]{:S(2)}, u32[]{:S(2)}) %collective-permute-start.23) | collective-permute-done | bytes 131104 | tf_op jit(solution)/shard_map/ppermute | solution.py:28
  390.1 18.8 %collective-permute-done.47 = bf16[64,1024]{1,0:T(8,128)(2,1)S(1)} collective-permute-done((bf16[64,1024]{1,0:T(8,128)(2,1)S(1)}, bf16[64,1024]{1,0:T(8,128)(2,1)S(1)}, u32[]{:S(2)}, u32[]{:S(2)}) %collective-permute-start.47) | collective-permute-done | bytes 131104 | tf_op jit(solution)/shard_map/ppermute | solution.py:28
  416.2 14.0 %collective-permute-done.14 = bf16[2,64,1536]{2,1,0:T(8,128)(2,1)S(1)} collective-permute-done((bf16[2,64,1536]{2,1,0:T(8,128)(2,1)S(1)}, bf16[2,64,1536]{2,1,0:T(8,128)(2,1)S(1)}, u32[]{:S(2)}, u32[]{:S(2)}) %collective-permute-start.14) | collective-permute-done | bytes 393248 | tf_op jit(solution)/shard_map/ppermute | solution.py:28
  430.4 5.8 %collective-permute-start.15 = (bf16[64,1536]{1,0:T(8,128)(2,1)S(1)}, bf16[64,1536]{1,0:T(8,128)(2,1)S(1)}, u32[]{:S(2)}, u32[]{:S(2)}) collective-permute-start(bf16[64,1536]{1,0:T(8,128)(2,1)S(1)} %dynamic-slice_bitcast_fusion.15), channel_id=1, source_target_pairs={{0,4},{1,5},{2,6},{3,7},{4,0},{5,1},{6,2},{7,3},{8,12},{9,13},{10,... | collective-permute-start | bytes 589832 | tf_op jit(solution)/shard_map/ppermute | solution.py:28
  (209 shorter events, 145.6 us)
Async XLA Ops:
  43.0 61.1 %collective-permute-start.10 = (bf16[2,2,64,1024]{3,2,1,0:T(8,128)(2,1)S(1)}, bf16[2,2,64,1024]{3,2,1,0:T(8,128)(2,1)S(1)}, u32[]{:S(2)}, u32[]{:S(2)}) collective-permute-start(bf16[2,2,64,1024]{3,2,1,0:T(8,128)(2,1)S(1)} %pad_maximum_fusion.26), channel_id=1, source_target_pairs={{0,1},{1,0},{2,3},{3,2},{4,5},{5,4},{6,7},{7,6},{8,9},{9,8},{10,11... | collective-permute-start | bytes 1572872 | tf_op jit(solution)/shard_map/ppermute | solution.py:40
  51.0 35.5 %collective-permute-start.5 = (bf16[2,64,1536]{2,1,0:T(8,128)(2,1)S(1)}, bf16[2,64,1536]{2,1,0:T(8,128)(2,1)S(1)}, u32[]{:S(2)}, u32[]{:S(2)}) collective-permute-start(bf16[2,64,1536]{2,1,0:T(8,128)(2,1)S(1)} %pad_maximum_fusion.29), channel_id=1, source_target_pairs={{0,8},{1,9},{2,10},{3,11},{4,12},{5,13},{6,14},{7,15},{8,0},{9,1},... | collective-permute-start | bytes 1179656 | tf_op jit(solution)/shard_map/ppermute | solution.py:40
  52.0 42.9 %collective-permute-start.25 = (bf16[2,64,1536]{2,1,0:T(8,128)(2,1)S(1)}, bf16[2,64,1536]{2,1,0:T(8,128)(2,1)S(1)}, u32[]{:S(2)}, u32[]{:S(2)}) collective-permute-start(bf16[2,64,1536]{2,1,0:T(8,128)(2,1)S(1)} %pad_maximum_fusion.30), channel_id=1, source_target_pairs={{0,8},{1,9},{2,10},{3,11},{4,12},{5,13},{6,14},{7,15},{8,0},{9,1},... | collective-permute-start | bytes 1179656 | tf_op jit(solution)/shard_map/ppermute | solution.py:40
  54.1 49.0 %collective-permute-start.29 = (bf16[2,64,1536]{2,1,0:T(8,128)(2,1)S(1)}, bf16[2,64,1536]{2,1,0:T(8,128)(2,1)S(1)}, u32[]{:S(2)}, u32[]{:S(2)}) collective-permute-start(bf16[2,64,1536]{2,1,0:T(8,128)(2,1)S(1)} %pad_maximum_fusion.31), channel_id=1, source_target_pairs={{0,8},{1,9},{2,10},{3,11},{4,12},{5,13},{6,14},{7,15},{8,0},{9,1},... | collective-permute-start | bytes 1179656 | tf_op jit(solution)/shard_map/ppermute | solution.py:40
  55.2 50.6 %collective-permute-start.34 = (bf16[2,2,64,1024]{3,2,1,0:T(8,128)(2,1)S(1)}, bf16[2,2,64,1024]{3,2,1,0:T(8,128)(2,1)S(1)}, u32[]{:S(2)}, u32[]{:S(2)}) collective-permute-start(bf16[2,2,64,1024]{3,2,1,0:T(8,128)(2,1)S(1)} %pad_maximum_fusion.27), channel_id=1, source_target_pairs={{0,1},{1,0},{2,3},{3,2},{4,5},{5,4},{6,7},{7,6},{8,9},{9,8},{10,11... | collective-permute-start | bytes 1572872 | tf_op jit(solution)/shard_map/ppermute | solution.py:40
  106.1 46.7 %collective-permute-start.35 = (bf16[2,2,2,64,1024]{4,3,2,1,0:T(8,128)(2,1)S(1)}, bf16[2,2,2,64,1024]{4,3,2,1,0:T(8,128)(2,1)S(1)}, u32[]{:S(2)}, u32[]{:S(2)}) collective-permute-start(bf16[2,2,2,64,1024]{4,3,2,1,0:T(8,128)(2,1)S(1)} %pad_maximum_fusion.21), channel_id=1, source_target_pairs={{0,4},{1,5},{2,6},{3,7},{4,0},{5,1},{6,2},{7,3},{8,12},{9,13},{10,... | collective-permute-start | bytes 3145736 | tf_op jit(solution)/shard_map/ppermute | solution.py:40
  115.3 50.6 %collective-permute-start.3 = (bf16[2,2,2,64,1536]{4,3,2,1,0:T(8,128)(2,1)S(1)}, bf16[2,2,2,64,1536]{4,3,2,1,0:T(8,128)(2,1)S(1)}, u32[]{:S(2)}, u32[]{:S(2)}) collective-permute-start(bf16[2,2,2,64,1536]{4,3,2,1,0:T(8,128)(2,1)S(1)} %pad_maximum_fusion.16), channel_id=1, source_target_pairs={{0,1},{1,0},{2,3},{3,2},{4,5},{5,4},{6,7},{7,6},{8,9},{9,8},{10,11... | collective-permute-start | bytes 4718600 | tf_op jit(solution)/shard_map/ppermute | solution.py:40
  122.9 43.5 %collective-permute-start.7 = (bf16[2,2,2,64,1536]{4,3,1,0,2:T(8,128)(2,1)S(1)}, bf16[2,2,2,64,1536]{4,3,1,0,2:T(8,128)(2,1)S(1)}, u32[]{:S(2)}, u32[]{:S(2)}) collective-permute-start(bf16[2,2,2,64,1536]{4,3,1,0,2:T(8,128)(2,1)S(1)} %pad_maximum_fusion.17), channel_id=1, source_target_pairs={{0,2},{1,3},{2,0},{3,1},{4,6},{5,7},{6,4},{7,5},{8,10},{9,11},{10,... | collective-permute-start | bytes 4718600 | tf_op jit(solution)/shard_map/ppermute | solution.py:40
  132.2 66.4 %collective-permute-start.27 = (bf16[2,2,2,64,1536]{4,3,2,1,0:T(8,128)(2,1)S(1)}, bf16[2,2,2,64,1536]{4,3,2,1,0:T(8,128)(2,1)}, u32[]{:S(2)}, u32[]{:S(2)}) collective-permute-start(bf16[2,2,2,64,1536]{4,3,2,1,0:T(8,128)(2,1)S(1)} %pad_maximum_fusion.18), channel_id=1, source_target_pairs={{0,1},{1,0},{2,3},{3,2},{4,5},{5,4},{6,7},{7,6},{8,9},{9,8},{10,11... | collective-permute-start | bytes 4718600 | tf_op jit(solution)/shard_map/ppermute | solution.py:40
  133.9 77.8 %collective-permute-start.31 = (bf16[2,2,2,64,1536]{4,3,1,0,2:T(8,128)(2,1)S(1)}, bf16[2,2,2,64,1536]{4,3,1,0,2:T(8,128)(2,1)}, u32[]{:S(2)}, u32[]{:S(2)}) collective-permute-start(bf16[2,2,2,64,1536]{4,3,1,0,2:T(8,128)(2,1)S(1)} %pad_maximum_fusion.19), channel_id=1, source_target_pairs={{0,2},{1,3},{2,0},{3,1},{4,6},{5,7},{6,4},{7,5},{8,10},{9,11},{10,... | collective-permute-start | bytes 4718600 | tf_op jit(solution)/shard_map/ppermute | solution.py:40
  245.1 92.3 %collective-permute-start.12 = (bf16[2,2,2,64,1536]{4,3,1,0,2:T(8,128)(2,1)S(1)}, bf16[2,2,2,64,1536]{4,3,1,0,2:T(8,128)(2,1)S(1)}, u32[]{:S(2)}, u32[]{:S(2)}) collective-permute-start(bf16[2,2,2,64,1536]{4,3,1,0,2:T(8,128)(2,1)S(1)} %bitcast.312), channel_id=1, source_target_pairs={{0,1},{1,0},{2,3},{3,2},{4,5},{5,4},{6,7},{7,6},{8,9},{9,8},{10,11... | collective-permute-start | bytes 4718600 | tf_op jit(solution)/shard_map/ppermute | solution.py:28
  247.0 92.5 %collective-permute-start.16 = (bf16[2,2,2,64,1536]{4,3,1,0,2:T(8,128)(2,1)S(1)}, bf16[2,2,2,64,1536]{4,3,1,0,2:T(8,128)(2,1)S(1)}, u32[]{:S(2)}, u32[]{:S(2)}) collective-permute-start(bf16[2,2,2,64,1536]{4,3,1,0,2:T(8,128)(2,1)S(1)} %bitcast.311), channel_id=1, source_target_pairs={{0,2},{1,3},{2,0},{3,1},{4,6},{5,7},{6,4},{7,5},{8,10},{9,11},{10,... | collective-permute-start | bytes 4718600 | tf_op jit(solution)/shard_map/ppermute | solution.py:28
  249.1 45.9 %collective-permute-start.44 = (bf16[2,2,2,64,1024]{4,3,0,1,2:T(8,128)(2,1)S(1)}, bf16[2,2,2,64,1024]{4,3,0,1,2:T(8,128)(2,1)S(1)}, u32[]{:S(2)}, u32[]{:S(2)}) collective-permute-start(bf16[2,2,2,64,1024]{4,3,0,1,2:T(8,128)(2,1)S(1)} %bitcast.315), channel_id=1, source_target_pairs={{0,4},{1,5},{2,6},{3,7},{4,0},{5,1},{6,2},{7,3},{8,12},{9,13},{10,... | collective-permute-start | bytes 3145736 | tf_op jit(solution)/shard_map/ppermute | solution.py:28
  251.5 89.1 %collective-permute-start.36 = (bf16[2,2,2,64,1536]{4,3,1,0,2:T(8,128)(2,1)S(1)}, bf16[2,2,2,64,1536]{4,3,1,0,2:T(8,128)(2,1)S(1)}, u32[]{:S(2)}, u32[]{:S(2)}) collective-permute-start(bf16[2,2,2,64,1536]{4,3,1,0,2:T(8,128)(2,1)S(1)} %bitcast.313), channel_id=1, source_target_pairs={{0,1},{1,0},{2,3},{3,2},{4,5},{5,4},{6,7},{7,6},{8,9},{9,8},{10,11... | collective-permute-start | bytes 4718600 | tf_op jit(solution)/shard_map/ppermute | solution.py:28
  275.4 52.1 %collective-permute-start.21 = (bf16[2,2,64,1024]{3,2,0,1:T(8,128)(2,1)S(1)}, bf16[2,2,64,1024]{3,2,0,1:T(8,128)(2,1)S(1)}, u32[]{:S(2)}, u32[]{:S(2)}) collective-permute-start(bf16[2,2,64,1024]{3,2,0,1:T(8,128)(2,1)S(1)} %dynamic-slice_bitcast_fusion.5), channel_id=1, source_target_pairs={{0,1},{1,0},{2,3},{3,2},{4,5},{5,4},{6,7},{7,6},{8,9},{9,8},{10,11... | collective-permute-start | bytes 1572872 | tf_op jit(solution)/shard_map/ppermute | solution.py:28
  295.5 41.1 %collective-permute-start.45 = (bf16[2,2,64,1024]{3,2,0,1:T(8,128)(2,1)S(1)}, bf16[2,2,64,1024]{3,2,0,1:T(8,128)(2,1)S(1)}, u32[]{:S(2)}, u32[]{:S(2)}) collective-permute-start(bf16[2,2,64,1024]{3,2,0,1:T(8,128)(2,1)S(1)} %dynamic-slice_bitcast_fusion.4), channel_id=1, source_target_pairs={{0,1},{1,0},{2,3},{3,2},{4,5},{5,4},{6,7},{7,6},{8,9},{9,8},{10,11... | collective-permute-start | bytes 1572872 | tf_op jit(solution)/shard_map/ppermute | solution.py:28
  327.5 37.3 %collective-permute-start.40 = (bf16[2,2,2,64,1536]{4,3,1,0,2:T(8,128)(2,1)S(1)}, bf16[2,2,2,64,1536]{4,3,1,0,2:T(8,128)(2,1)S(1)}, u32[]{:S(2)}, u32[]{:S(2)}) collective-permute-start(bf16[2,2,2,64,1536]{4,3,1,0,2:T(8,128)(2,1)S(1)} %bitcast.314), channel_id=1, source_target_pairs={{0,2},{1,3},{2,0},{3,1},{4,6},{5,7},{6,4},{7,5},{8,10},{9,11},{10,... | collective-permute-start | bytes 4718600 | tf_op jit(solution)/shard_map/ppermute | solution.py:28
  336.6 33.8 %collective-permute-start.22 = (bf16[2,64,1024]{2,1,0:T(8,128)(2,1)S(1)}, bf16[2,64,1024]{2,1,0:T(8,128)(2,1)S(1)}, u32[]{:S(2)}, u32[]{:S(2)}) collective-permute-start(bf16[2,64,1024]{2,1,0:T(8,128)(2,1)S(1)} %dynamic-slice_bitcast_fusion.11), channel_id=1, source_target_pairs={{0,2},{1,3},{2,0},{3,1},{4,6},{5,7},{6,4},{7,5},{8,10},{9,11},{10,... | collective-permute-start | bytes 786440 | tf_op jit(solution)/shard_map/ppermute | solution.py:28
  337.5 38.6 %collective-permute-start.46 = (bf16[2,64,1024]{2,1,0:T(8,128)(2,1)S(1)}, bf16[2,64,1024]{2,1,0:T(8,128)(2,1)S(1)}, u32[]{:S(2)}, u32[]{:S(2)}) collective-permute-start(bf16[2,64,1024]{2,1,0:T(8,128)(2,1)S(1)} %dynamic-slice_bitcast_fusion.10), channel_id=1, source_target_pairs={{0,2},{1,3},{2,0},{3,1},{4,6},{5,7},{6,4},{7,5},{8,10},{9,11},{10,... | collective-permute-start | bytes 786440 | tf_op jit(solution)/shard_map/ppermute | solution.py:28
  339.5 69.5 %collective-permute-start.13 = (bf16[2,2,64,1536]{3,2,1,0:T(8,128)(2,1)S(1)}, bf16[2,2,64,1536]{3,2,1,0:T(8,128)(2,1)S(1)}, u32[]{:S(2)}, u32[]{:S(2)}) collective-permute-start(bf16[2,2,64,1536]{3,2,1,0:T(8,128)(2,1)S(1)} %dynamic-slice_bitcast_fusion.3), channel_id=1, source_target_pairs={{0,2},{1,3},{2,0},{3,1},{4,6},{5,7},{6,4},{7,5},{8,10},{9,11},{10,... | collective-permute-start | bytes 2359304 | tf_op jit(solution)/shard_map/ppermute | solution.py:28
  340.6 68.7 %collective-permute-start.17 = (bf16[2,2,64,1536]{3,2,1,0:T(8,128)(2,1)S(1)}, bf16[2,2,64,1536]{3,2,1,0:T(8,128)(2,1)S(1)}, u32[]{:S(2)}, u32[]{:S(2)}) collective-permute-start(bf16[2,2,64,1536]{3,2,1,0:T(8,128)(2,1)S(1)} %dynamic-slice_bitcast_fusion.2), channel_id=1, source_target_pairs={{0,1},{1,0},{2,3},{3,2},{4,5},{5,4},{6,7},{7,6},{8,9},{9,8},{10,11... | collective-permute-start | bytes 2359304 | tf_op jit(solution)/shard_map/ppermute | solution.py:28
  364.8 47.8 %collective-permute-start.37 = (bf16[2,2,64,1536]{3,2,1,0:T(8,128)(2,1)S(1)}, bf16[2,2,64,1536]{3,2,1,0:T(8,128)(2,1)S(1)}, u32[]{:S(2)}, u32[]{:S(2)}) collective-permute-start(bf16[2,2,64,1536]{3,2,1,0:T(8,128)(2,1)S(1)} %dynamic-slice_bitcast_fusion.1), channel_id=1, source_target_pairs={{0,2},{1,3},{2,0},{3,1},{4,6},{5,7},{6,4},{7,5},{8,10},{9,11},{10,... | collective-permute-start | bytes 2359304 | tf_op jit(solution)/shard_map/ppermute | solution.py:28
  370.4 42.6 %collective-permute-start.41 = (bf16[2,2,64,1536]{3,2,1,0:T(8,128)(2,1)S(1)}, bf16[2,2,64,1536]{3,2,1,0:T(8,128)(2,1)S(1)}, u32[]{:S(2)}, u32[]{:S(2)}) collective-permute-start(bf16[2,2,64,1536]{3,2,1,0:T(8,128)(2,1)S(1)} %dynamic-slice_bitcast_fusion), channel_id=1, source_target_pairs={{0,1},{1,0},{2,3},{3,2},{4,5},{5,4},{6,7},{7,6},{8,9},{9,8},{10,11... | collective-permute-start | bytes 2359304 | tf_op jit(solution)/shard_map/ppermute | solution.py:28
  413.2 36.1 %collective-permute-start.42 = (bf16[2,64,1536]{2,1,0:T(8,128)(2,1)S(1)}, bf16[2,64,1536]{2,1,0:T(8,128)(2,1)S(1)}, u32[]{:S(2)}, u32[]{:S(2)}) collective-permute-start(bf16[2,64,1536]{2,1,0:T(8,128)(2,1)S(1)} %dynamic-slice_bitcast_fusion.6), channel_id=1, source_target_pairs={{0,8},{1,9},{2,10},{3,11},{4,12},{5,13},{6,14},{7,15},{8,0},{9,1},... | collective-permute-start | bytes 1179656 | tf_op jit(solution)/shard_map/ppermute | solution.py:28
  (31 other events, 521.8 us)
